TPU v7x, 512 devices: a whole 4x8x8 slice. The times are simulated.
512 devices in a mesh: rep: 16 (over y, core), vol: 32 (over z, x).
Axes of the slice: x: 4, y: 8, z: 8, core: 2. Of those that a mesh axis runs over, the one named last changes fastest.
Arguments:
- positions: float32 [131072, 2, 24], P(('rep', 'vol')), may hold values from -1 to 1
- spacing: float32 [131072, 2, 8], P(('rep', 'vol')), may hold values from 0.05 to 0.5
- volume_ids: int32 [131072, 2], P(('rep', 'vol')), may hold values from 0 to 127, all different within a row; in each aligned block of 256 rows (0 to 255, 256 to 511, ...) at most 8 rows name the same one
- target: float32 [3, 131072], P(None, ('rep', 'vol')), may hold values from 0 to 1
- w_in: bfloat16 [128, 64, 256], P('vol'), may hold values from -0.75 to 0.75
- w_hidden: bfloat16 [128, 256, 256], P('vol'), may hold values from -0.375 to 0.375
- w_head: bfloat16 [128, 4, 256], P('vol'), may hold values from -0.375 to 0.375
Outputs:
- rendered: float32 [3, 131072], P(None, ('rep', 'vol'))
- grad_in: float32 [128, 64, 256], P('vol', None, 'rep')
- grad_hidden: float32 [128, 256, 256], P('vol', 'rep')
- grad_head: float32 [128, 4, 256], P('vol', None, 'rep')
Inputs may be any that keep to these rules, and one draw needn't show every extreme that they name: `volume_ids`: the 2 entries of a ray are different sub-volumes, nearest first. Among the 256 rays of one device no sub-volume is named more than 8 times, and in some device's rays one is named exactly 8 times.
All inputs are finite; a program needn't handle non-finite values.
Results may differ from a plain program's by a relative error of at most 0.012.
Values may be sent and summed in bfloat16 or wider, within the bound.
A program may use at most 64 MiB of HBM per device.

v0:
```python
import math

import jax
import jax.numpy as jnp
from jax import lax
from jax.sharding import PartitionSpec as P

FREQS = 10
ENC = 64


def encode(points):
    coords = jnp.swapaxes(points, -1, -2)
    scales = (2.0 ** jnp.arange(FREQS)).astype(jnp.float32) * math.pi
    angles = (coords[..., None] * scales).reshape(coords.shape[:-1] + (3 * FREQS,))
    unit = jnp.ones(coords.shape[:-1] + (1,), jnp.float32)
    return jnp.concatenate([jnp.sin(angles), jnp.cos(angles), coords, unit], axis=-1)


def silu_slope(pre_act):
    gate = jax.nn.sigmoid(pre_act)
    return gate * (1.0 + pre_act * (1.0 - gate))


def product(left, right):
    return jnp.dot(left, right, preferred_element_type=jnp.float32)


def forward(rows, w_first, w_mid, w_last):
    pre_one = product(rows, w_first)
    act_one = jax.nn.silu(pre_one).astype(jnp.bfloat16)
    pre_two = product(act_one, w_mid)
    act_two = jax.nn.silu(pre_two).astype(jnp.bfloat16)
    raw_out = product(act_two, w_last.T)
    return (pre_one, act_one, pre_two, act_two, raw_out)


def activate(raw_out):
    return jnp.concatenate(
        [jax.nn.sigmoid(raw_out[:, :3]), jax.nn.softplus(raw_out[:, 3:])], axis=1
    )


def backward(rows, cotangent, w_first, w_mid, w_last):
    pre_one, act_one, pre_two, act_two, raw_out = forward(rows, w_first, w_mid, w_last)
    gate = jax.nn.sigmoid(raw_out)
    slope = jnp.concatenate([gate[:, :3] * (1.0 - gate[:, :3]), gate[:, 3:]], axis=1)
    cot_raw = (cotangent * slope).astype(jnp.bfloat16)
    d_last = product(cot_raw.T, act_two)
    cot_two = (product(cot_raw, w_last) * silu_slope(pre_two)).astype(jnp.bfloat16)
    d_mid = product(act_one.T, cot_two)
    cot_one = (product(cot_two, w_mid.T) * silu_slope(pre_one)).astype(jnp.bfloat16)
    d_first = product(rows.T, cot_one)
    return (d_first, d_mid, d_last)


def slots_of(volume_ids, volume_count, capacity):
    flat_ids = volume_ids.reshape(-1)
    table = (flat_ids[:, None] == jnp.arange(volume_count, dtype=jnp.int32)[None, :]).astype(
        jnp.int32
    )
    earlier = jnp.cumsum(table, axis=0) - table
    return flat_ids * capacity + jnp.sum(earlier * table, axis=1)


def segment_values(radiance, spacing):
    tau = radiance[..., 3] * spacing
    alpha = 1.0 - jnp.exp(-tau)
    before = jnp.cumsum(tau, axis=-1) - tau
    share = jnp.exp(-before) * alpha
    seg_color = jnp.sum(share[..., None] * radiance[..., :3], axis=-2)
    passing = jnp.exp(-jnp.sum(tau, axis=-1))
    return jnp.concatenate([seg_color, passing[..., None]], axis=-1)


def combine(per_seg):
    color = per_seg[:, 0, :3]
    carried = per_seg[:, 0, 3]
    color = color + carried[:, None] * per_seg[:, 1, :3]
    return color.T


def local(positions, spacing, volume_ids, target, w_in, w_hidden, w_head):
    ray_count, seg_count = volume_ids.shape
    sample_count = spacing.shape[2]
    owners = lax.axis_size("vol")
    held_count = w_in.shape[0]
    volume_count = owners * held_count
    capacity = 2 * ray_count * seg_count // volume_count
    row_count = owners * capacity * sample_count
    places = slots_of(volume_ids, volume_count, capacity)
    gap_slots = (
        jnp.zeros((volume_count * capacity, sample_count), jnp.float32)
        .at[places]
        .set(spacing.reshape(ray_count * seg_count, sample_count))
    )
    gap_slots = gap_slots.reshape(owners, held_count * capacity, sample_count)
    points = positions.reshape(ray_count * seg_count, 3, sample_count)
    feats = encode(points).astype(jnp.bfloat16).reshape(ray_count * seg_count, sample_count * ENC)
    outgoing = (
        jnp.zeros((volume_count * capacity, sample_count * ENC), jnp.bfloat16).at[places].set(feats)
    )
    outgoing = outgoing.reshape(owners, held_count * capacity, sample_count * ENC)
    arrived, gap_arrived = (
        lax.all_to_all(outgoing, "vol", split_axis=0, concat_axis=0, tiled=True),
        lax.all_to_all(
            gap_slots.astype(jnp.bfloat16), "vol", split_axis=0, concat_axis=0, tiled=True
        ).astype(gap_slots.dtype),
    )
    features = arrived.reshape(owners, held_count, capacity * sample_count, ENC)
    rows = jnp.swapaxes(features, 0, 1).reshape(held_count, row_count, ENC)
    radiance = lax.map(lambda item: activate(forward(*item)[4]), (rows, w_in, w_hidden, w_head))
    gaps_here = jnp.swapaxes(gap_arrived.reshape(owners, held_count, capacity, sample_count), 0, 1)
    samples_here = radiance.reshape(held_count, owners, capacity, sample_count, 4)
    seg_here, seg_pull = jax.vjp(lambda values: segment_values(values, gaps_here), samples_here)
    leaving = jnp.swapaxes(seg_here, 0, 1).reshape(owners, held_count * capacity, 4)
    returned = lax.all_to_all(leaving, "vol", split_axis=0, concat_axis=0, tiled=True)
    per_seg = returned.reshape(volume_count * capacity, 4)[places].reshape(ray_count, seg_count, 4)
    color, pull = jax.vjp(combine, per_seg)
    (cot_seg,) = pull((color - target) / lax.axis_size("rep"))
    cot_out = (
        jnp.zeros((volume_count * capacity, 4), jnp.float32)
        .at[places]
        .set(cot_seg.reshape(ray_count * seg_count, 4))
    )
    cot_back = lax.all_to_all(
        cot_out.reshape(owners, held_count * capacity, 4),
        "vol",
        split_axis=0,
        concat_axis=0,
        tiled=True,
    )
    cot_here = jnp.swapaxes(cot_back.reshape(owners, held_count, capacity, 4), 0, 1)
    (cot_samples,) = seg_pull(cot_here)
    cot_rows = cot_samples.reshape(held_count, row_count, 4)
    partial_grads = lax.map(lambda item: backward(*item), (rows, cot_rows, w_in, w_hidden, w_head))
    grad_in, grad_hidden, grad_head = (
        lax.psum_scatter(partial_grads[0], "rep", scatter_dimension=2, tiled=True),
        lax.psum_scatter(partial_grads[1], "rep", scatter_dimension=1, tiled=True),
        lax.psum_scatter(partial_grads[2], "rep", scatter_dimension=2, tiled=True),
    )
    return (color, grad_in, grad_hidden, grad_head)


def solution(mesh):
    return jax.shard_map(
        local,
        mesh=mesh,
        in_specs=(
            P(("rep", "vol"), None, None),
            P(("rep", "vol"), None, None),
            P(("rep", "vol"), None),
            P(None, ("rep", "vol")),
            P("vol", None, None),
            P("vol", None, None),
            P("vol", None, None),
        ),
        out_specs=(
            P(None, ("rep", "vol")),
            P("vol", None, "rep"),
            P("vol", "rep", None),
            P("vol", None, "rep"),
        ),
        check_vma=False,
    )
```

profile of v0, /device:TPU:1, one launch (start us, length us, event | category | flops | bytes accessed | tf_op | source)
XLA Modules:
  0.0 392.2 jit_solution(17867927194776383264)
XLA Ops:
  13.0 13.7 %all-to-all-start.1 = ((bf16[32,2,128]{2,1,0:T(2,128)(2,1)}), bf16[32,2,128]{2,1,0:T(2,128)(2,1)S(1)}, u32[]{:S(2)}, u32[]{:S(2)}) async-start(bf16[32,2,128]{2,1,0:T(2,128)(2,1)} %reshape.194), calls=%async_computation.1 | async-start | bytes 32768 | tf_op jit(solution)/shard_map/all_to_all | solution.py:106
  30.2 3.5 scatter_custom_fusion
  35.2 7.9 %all-to-all-start = ((bf16[32,32,512]{2,1,0:T(8,128)(2,1)}), bf16[32,32,512]{2,1,0:T(8,128)(2,1)S(1)}, u32[]{:S(2)}, u32[]{:S(2)}) async-start(bf16[32,32,512]{2,1,0:T(8,128)(2,1)} %bitcast.24), calls=%async_computation | async-start | bytes 2097152 | tf_op jit(solution)/shard_map/all_to_all | solution.py:105
  44.3 24.2 %all-to-all-done = bf16[32,32,512]{2,1,0:T(8,128)(2,1)S(1)} async-done(((bf16[32,32,512]{2,1,0:T(8,128)(2,1)}), bf16[32,32,512]{2,1,0:T(8,128)(2,1)S(1)}, u32[]{:S(2)}, u32[]{:S(2)}) %all-to-all-start) | async-done | bytes 1048608 | tf_op jit(solution)/shard_map/all_to_all | solution.py:105
  72.5 10.7 %while.24 = (s32[]{:T(128)}, f32[4,2048,4]{1,2,0:T(4,128)S(1)}, bf16[4,2048,64]{2,1,0:T(8,128)(2,1)S(1)}, bf16[4,64,256]{2,1,0:T(8,128)(2,1)}, bf16[4,256,256]{2...) while((s32[]{:T(128)}, f32[4,2048,4]{1,2,0:T(4,128)S(1)}, bf16[4,2048,64]{2,1,0:T(8,128)(2,1)S(1)}, ...), condition=%wide.region_5.6_spmd, body=%wide.region_4.5_spmd.sunk | while | flops 345020416 | bytes 2960981 | solution.py:112
  72.5 2.2 multiply_convert_fusion.9
  75.2 2.2 multiply_convert_fusion.9
  77.9 2.2 multiply_convert_fusion.9
  80.6 2.2 multiply_convert_fusion.9
  86.0 20.3 %reduce_window_sum.39 = f32[4,32,8,8]{3,2,1,0:T(8,128)S(1)} reduce-window(f32[4,32,8,8]{3,2,1,0:T(8,128)S(1)} %get-tuple-element.212, f32[]{:T(128)} %constant.53.clone.1), window={size=1x1x1x8 pad=0_0x0_0x0_0x7_0}, to_apply=%region_7.8 | reduce-window | flops 57344 | bytes 65540 | tf_op jit(solution)/shard_map/jvp(jit(cumsum))/reduce_window_sum | solution.py:69
  109.8 6.7 %all-to-all-start.2 = ((f32[32,1,128]{2,1,0:T(1,128)}), f32[32,1,128]{2,1,0:T(1,128)S(1)}, u32[]{:S(2)}, u32[]{:S(2)}) async-start(f32[32,1,128]{2,1,0:T(1,128)} %reshape.196), calls=%async_computation.2 | async-start | bytes 32768 | tf_op jit(solution)/shard_map/all_to_all | solution.py:117
  116.5 8.5 %all-to-all-done.2 = f32[32,1,128]{2,1,0:T(1,128)S(1)} async-done(((f32[32,1,128]{2,1,0:T(1,128)}), f32[32,1,128]{2,1,0:T(1,128)S(1)}, u32[]{:S(2)}, u32[]{:S(2)}) %all-to-all-start.2) | async-done | bytes 16416 | tf_op jit(solution)/shard_map/all_to_all | solution.py:117
  131.5 3.8 all-to-all-start.3
  135.6 8.2 %all-to-all-done.3 = f32[32,1,128]{2,1,0:T(1,128)S(1)} async-done(((f32[32,1,128]{2,1,0:T(1,128)}), f32[32,1,128]{2,1,0:T(1,128)S(1)}, u32[]{:S(2)}, u32[]{:S(2)}) %all-to-all-start.3) | async-done | bytes 16416 | tf_op jit(solution)/shard_map/all_to_all | solution.py:126
  144.8 3.6 broadcast_multiply_fusion
  149.7 20.3 %reduce_window_sum.40 = f32[4,32,8,8]{3,2,1,0:T(8,128)S(1)} reduce-window(f32[4,32,8,8]{3,2,1,0:T(8,128)S(1)} %fusion.70, f32[]{:T(128)} %constant.53.clone.1), window={size=1x1x1x8 pad=0_0x0_0x0_0x0_7}, to_apply=%region_13.14 | reduce-window | flops 57344 | bytes 65540 | tf_op jit(solution)/shard_map/transpose(jvp(jit(cumsum)))/reduce_window_sum | solution.py:69
  172.9 33.0 %while.25 = (s32[]{:T(128)}, f32[4,64,256]{2,1,0:T(8,128)S(1)}, f32[4,256,256]{2,1,0:T(8,128)}, f32[4,4,256]{2,1,0:T(4,128)S(1)}, bf16[4,2048,64]{2,1,0:T(8,128)...) while((s32[]{:T(128)}, f32[4,64,256]{2,1,0:T(8,128)S(1)}, ...), condition=%wide.region_15.16_spmd, body=%wide.region_14.15_spmd.sunk | while | flops 969494528 | bytes 25031816 | solution.py:136
  178.7 2.5 fusion.155
  186.9 2.5 fusion.155
  195.2 2.5 fusion.155
  203.5 2.5 fusion.155
  208.9 53.2 %reduce-scatter.10.cloned.1.call-done = f32[16,16]{1,0:T(8,128)} async-done(((f32[256,16]{1,0:T(8,128)}), f32[16,16]{1,0:T(8,128)}) %reduce-scatter.10.cloned.1.call-update) | async-done | bytes 1040
  263.7 60.0 %reduce-scatter.6.cloned.1.call-done = f32[4,64,16]{1,2,0:T(8,128)} async-done(((f32[4,64,256]{1,2,0:T(8,128)}), f32[4,64,16]{1,2,0:T(8,128)}) %reduce-scatter.6.cloned.1.call-update) | async-done | bytes 16400 | tf_op jit(solution)/shard_map/reduce_scatter | solution.py:138
  323.6 62.0 %reduce-scatter.8.cloned.1.call-done = f32[4,16,256]{2,1,0:T(8,128)} async-done(((f32[4,256,256]{2,1,0:T(8,128)}), f32[4,16,256]{2,1,0:T(8,128)}) %reduce-scatter.8.cloned.1.call-update) | async-done | bytes 65552 | tf_op jit(solution)/shard_map/reduce_scatter | solution.py:139
  (176 shorter events, 62.9 us)
Async XLA Ops:
  7.2 2.6 copy-start.11
  7.2 19.5 %copy-start.8 = (f32[256,2,24]{0,2,1:T(8,128)S(1)}, f32[256,2,24]{0,2,1:T(8,128)}, u32[]{:S(2)}) copy-start(f32[256,2,24]{0,2,1:T(8,128)} %param.11) | copy-start | bytes 147460
  13.0 22.2 %all-to-all-start.1 = ((bf16[32,2,128]{2,1,0:T(2,128)(2,1)}), bf16[32,2,128]{2,1,0:T(2,128)(2,1)S(1)}, u32[]{:S(2)}, u32[]{:S(2)}) async-start(bf16[32,2,128]{2,1,0:T(2,128)(2,1)} %reshape.194), calls=%async_computation.1 | async-start | bytes 32768 | tf_op jit(solution)/shard_map/all_to_all | solution.py:106
  35.2 33.3 %all-to-all-start = ((bf16[32,32,512]{2,1,0:T(8,128)(2,1)}), bf16[32,32,512]{2,1,0:T(8,128)(2,1)S(1)}, u32[]{:S(2)}, u32[]{:S(2)}) async-start(bf16[32,32,512]{2,1,0:T(8,128)(2,1)} %bitcast.24), calls=%async_computation | async-start | bytes 2097152 | tf_op jit(solution)/shard_map/all_to_all | solution.py:105
  70.6 1.8 copy-start.7
  83.2 1.4 copy-start
  106.3 2.6 copy-start.1
  109.8 15.2 %all-to-all-start.2 = ((f32[32,1,128]{2,1,0:T(1,128)}), f32[32,1,128]{2,1,0:T(1,128)S(1)}, u32[]{:S(2)}, u32[]{:S(2)}) async-start(f32[32,1,128]{2,1,0:T(1,128)} %reshape.196), calls=%async_computation.2 | async-start | bytes 32768 | tf_op jit(solution)/shard_map/all_to_all | solution.py:117
  126.1 2.2 copy-start.9
  128.4 20.0 %copy-start.10 = (f32[3,256]{1,0:T(4,128)}, f32[3,256]{1,0:T(4,128)S(1)}, u32[]{:S(2)}) copy-start(f32[3,256]{1,0:T(4,128)S(1)} %get-tuple-element.210) | copy-start | bytes 9220
  131.5 12.4 %all-to-all-start.3 = ((f32[32,1,128]{2,1,0:T(1,128)}), f32[32,1,128]{2,1,0:T(1,128)S(1)}, u32[]{:S(2)}, u32[]{:S(2)}) async-start(f32[32,1,128]{2,1,0:T(1,128)} %reshape.198), calls=%async_computation.3 | async-start | bytes 32768 | tf_op jit(solution)/shard_map/all_to_all | solution.py:126
  135.3 126.9 %reduce-scatter.10.cloned.1.call-start = ((), (), s32[]{:S(2)}) async-start(), calls=%async_computation.9 | async-start | bytes 139264
  144.8 3.6 copy-start.2
  148.4 21.6 %copy-start.5 = (f32[32,4,8,8]{3,2,0,1:T(8,128)S(1)}, f32[32,4,8,8]{3,2,0,1:T(8,128)}, u32[]{:S(2)}) copy-start(f32[32,4,8,8]{3,2,0,1:T(8,128)} %copy.205) | copy-start | bytes 98308
  170.0 1.6 copy-start.3
  171.7 1.2 copy-start.6
  171.7 1.2 copy-start.12
  171.7 1.1 copy-start.13
  177.2 1.5 copy-start.14
  185.4 1.5 copy-start.14
  193.7 1.5 copy-start.14
  202.0 1.5 copy-start.14
  207.1 116.5 %reduce-scatter.6.cloned.1.call-start = ((), (), s32[]{:S(2)}) async-start(), calls=%async_computation.7 | async-start | bytes 557056 | tf_op jit(solution)/shard_map/reduce_scatter | solution.py:138
  208.2 177.4 %reduce-scatter.8.cloned.1.call-start = ((), (), s32[]{:S(2)}) async-start(), calls=%async_computation.8 | async-start | bytes 1114112 | tf_op jit(solution)/shard_map/reduce_scatter | solution.py:139
  (1 other events, 1.1 us)
Sparse Core Ops, SparseCore 0:
  207.3 54.8 reduce-scatter.9
  265.8 57.8 reduce-scatter.5
  327.0 58.5 reduce-scatter.7
where the time goes:
time: 394 us; the launch traced here: 392 us
  waiting for transfers between devices  218 us (55%)
  other arithmetic  54.9 us (14%)
  matrix products  42.7 us (11%)
  starting transfers between devices  32.4 us (8%)
  local copies, waits for them, and re-layouts  28.9 us (7%)
  between operations  14.3 us (4%)
    reduce_scatter x1, waiting for transfers between devices, local(): lax.psum_scatter(partial_grads[1], 'rep', scatter_dimension=1, tiled=True)  62 us
    reduce_scatter x1, waiting for transfers between devices, local(): lax.psum_scatter(partial_grads[0], 'rep', scatter_dimension=2, tiled=True)  60 us
    unnamed x4, waiting for transfers between devices  53.9 us
    dot_general x36, matrix products, product(): return jnp.dot(left, right, preferred_element_type=jnp.float32)  42.7 us
    another operation x2, other arithmetic, segment_values(): before = jnp.cumsum(tau, axis=-1) - tau  40.6 us
    all_to_all x1, waiting for transfers between devices, local(): lax.all_to_all(outgoing, 'vol', split_axis=0, concat_axis=0, tiled=True)  24.2 us
    all_to_all x1, starting transfers between devices, local(): lax.all_to_all(gap_slots.astype(jnp.bfloat16), 'vol', split_axis=0, conca...  13.7 us
    all_to_all x1, waiting for transfers between devices, local(): lax.all_to_all(leaving, 'vol', split_axis=0, concat_axis=0, tiled=True)  8.49 us
  transfers between devices with their start and end apart: 7, of which 7 were waited for; matrix products, arithmetic and copies ran while one was open for 3% of the time, Pallas kernels for 0%

commit v1 on v0

v1 whole, which is shorter than its diff:
```python
import functools
import math

import jax
import jax.numpy as jnp
from jax import lax
from jax.experimental import pallas as pl
from jax.experimental.pallas import tpu as pltpu
from jax.sharding import PartitionSpec as P

FREQS = 10
ENC = 64
WIDTH = 256
SAMPLES = 8
CAP = 8
HELD = 4
VALS = 4 * SAMPLES
PACK = 384
HALF = FREQS // 2
MESH = pl.DeviceIdType.MESH
BF16 = jnp.bfloat16
F32 = jnp.float32


def dot(left, right):
    return jnp.dot(left, right, preferred_element_type=F32)


def dot_nt(left, right):
    return lax.dot_general(left, right, (((1,), (1,)), ((), ())), preferred_element_type=F32)


def split3(x, axis):
    high = x.astype(BF16)
    rest = x - high.astype(F32)
    mid = rest.astype(BF16)
    low = (rest - mid.astype(F32)).astype(BF16)
    return jnp.concatenate([high, mid, low], axis=axis)


def sine_cosine(turns):
    x = turns * (math.pi / 2)
    y = x * x
    sin = jnp.full_like(y, 1.0 / math.factorial(13))
    for k in (11, 9, 7, 5, 3, 1):
        sin = (1.0 / math.factorial(k)) - y * sin
    sin = sin * x
    cos = jnp.full_like(y, 1.0 / math.factorial(12))
    for k in (10, 8, 6, 4, 2, 0):
        cos = (1.0 / math.factorial(k)) - y * cos
    return 2.0 * sin * cos, 1.0 - 2.0 * sin * sin


def sigmoid(x):
    return 1.0 / (1.0 + jnp.exp(-x))


def softplus(x):
    e = jnp.exp(-jnp.abs(x))
    small = e * (1.0 - e * (0.5 - e * (1.0 / 3.0)))
    return jnp.maximum(x, 0.0) + jnp.where(e < 1e-2, small, jnp.log(1.0 + e))


def one_hot(rows, row):
    spots = lax.broadcasted_iota(jnp.int32, (rows, row.shape[1]), 0)
    return jnp.where(spots == row, 1.0, 0.0)


def kernel(
    n_rep, n_vol, rays,
    pos, gap, ids, target, w_in, w_hidden, w_head,
    out_color, out_in, out_hidden, out_head,
    send_a, recv_a, send_b, recv_b, send_c, recv_c,
    table, feats, enc, act_one, act_two, slope_one, slope_two,
    raw_s, gap_s, cot_f, cot_two_s, cot_one_s, turn, table_t,
    w_in_t, w_hidden_t, w_head_p, w_head_t,
    part, pair_in, block_out, block_in, own_block,
    sem, pair_sem, block_sem,
):
    me_r, me_v = lax.axis_index("rep"), lax.axis_index("vol")
    n_y = n_rep // 2
    me_y, me_c = me_r // 2, lax.rem(me_r, 2)
    lanes = n_vol * CAP
    segs = 2 * rays
    volumes = n_vol * HELD
    rows = WIDTH // n_rep

    def vol_peer(k):
        return lax.rem(me_v + k, n_vol)

    def rep_peer(k):
        return lax.rem(me_y + k, n_y) * 2 + me_c

    sibling = me_y * 2 + 1 - me_c

    barrier = pltpu.get_barrier_semaphore()

    def greet_vol(k, carry):
        pl.semaphore_signal(barrier, inc=1, device_id=(me_r, vol_peer(k)), device_id_type=MESH)
        return carry

    def greet_rep(k, carry):
        pl.semaphore_signal(barrier, inc=1, device_id=(rep_peer(k), me_v), device_id_type=MESH)
        return carry

    lax.fori_loop(1, n_vol, greet_vol, 0)
    lax.fori_loop(1, n_y, greet_rep, 0)
    pl.semaphore_signal(barrier, inc=1, device_id=(sibling, me_v), device_id_type=MESH)

    id_row = jnp.concatenate([ids[0:1, :], ids[1:2, :]], axis=1)
    hot = one_hot(volumes, id_row)
    before = jnp.where(
        lax.broadcasted_iota(jnp.int32, (rays, rays), 0)
        < lax.broadcasted_iota(jnp.int32, (rays, rays), 1),
        1.0,
        0.0,
    ).astype(BF16)
    hot_0, hot_1 = hot[:, :rays], hot[:, rays:]
    earlier_0 = dot(hot_0.astype(BF16), before)
    earlier_1 = dot(hot_1.astype(BF16), before) + jnp.sum(hot_0, axis=1, keepdims=True)
    rank = jnp.concatenate(
        [
            jnp.sum(earlier_0 * hot_0, axis=0, keepdims=True),
            jnp.sum(earlier_1 * hot_1, axis=0, keepdims=True),
        ],
        axis=1,
    ).astype(jnp.int32)
    owner = lax.shift_right_logical(id_row, 2)
    held = lax.bitwise_and(id_row, 3)
    place_hot = one_hot(lanes, owner * CAP + rank).astype(BF16)
    vals = jnp.concatenate(
        [
            jnp.concatenate([pos[0], gap[0]], axis=0),
            jnp.concatenate([pos[1], gap[1]], axis=0),
        ],
        axis=1,
    )
    spread = jnp.concatenate([jnp.where(held == v, vals, 0.0) for v in range(HELD)], axis=0)
    moved = dot_nt(place_hot, split3(spread, 0))
    moved = (moved[:, 0:128] + moved[:, 128:256]) + moved[:, 256:384]
    send_a[...] = moved.reshape(n_vol, CAP, 128)
    recv_a[me_v] = send_a[me_v]
    pl.semaphore_wait(barrier, n_vol - 1 + n_y)

    def exchange(source, landing, number):
        def start(k, carry):
            peer = vol_peer(k)
            pltpu.make_async_remote_copy(
                src_ref=source.at[peer],
                dst_ref=landing.at[me_v],
                send_sem=sem.at[2 * number],
                recv_sem=sem.at[2 * number + 1],
                device_id=(me_r, peer),
                device_id_type=MESH,
            ).start()
            return carry

        lax.fori_loop(1, n_vol, start, 0)

    def await_all(buffer, which):
        span = buffer.at[pl.ds(0, n_vol - 1)]
        pltpu.make_async_copy(span, span, sem.at[which]).wait()

    exchange(send_a, recv_a, 0)

    cot_f[...] = jnp.zeros_like(cot_f)
    turn[...] = jnp.zeros_like(turn)
    w_head_p[...] = jnp.zeros_like(w_head_p)

    def turn_weights(v, carry):
        w_in_t[v] = w_in[v].astype(F32).T.astype(BF16)
        w_hidden_t[v] = w_hidden[v].astype(F32).T.astype(BF16)
        head = jnp.concatenate([w_head[v].astype(F32), jnp.zeros((124, WIDTH), F32)], axis=0)
        w_head_p[v] = head[0:16].astype(BF16)
        w_head_t[v] = head.T[:, 0:16].astype(BF16)
        return carry

    lax.fori_loop(0, HELD, turn_weights, 0)

    await_all(recv_a, 1)
    table[...] = recv_a[...].reshape(lanes, 128).T

    blocks, block = feats.shape[0], feats.shape[2]

    def put(at, values):
        for b in range(blocks):
            feats[b, at : at + values.shape[0], :] = values[:, b * block : (b + 1) * block]

    def forward(v, carry):
        base = pl.multiple_of(v * VALS, VALS)
        points = table[pl.ds(base, 24), :]
        gaps = table[pl.ds(base + 24, 8), :]
        wide = points * (2.0**HALF)
        wide = wide - 2.0 * jnp.floor(wide * 0.5 + 0.5)
        sin_lo, cos_lo = sine_cosine(points)
        sin_hi, cos_hi = sine_cosine(wide)
        for f in range(HALF):
            for offset, sin, cos in ((f, sin_lo, cos_lo), (HALF + f, sin_hi, cos_hi)):
                for c in range(3):
                    at = c * FREQS + offset
                    put(at * 8, sin[c * 8 : c * 8 + 8])
                    put((30 + at) * 8, cos[c * 8 : c * 8 + 8])
            sin_lo, cos_lo = 2.0 * sin_lo * cos_lo, 1.0 - 2.0 * sin_lo * sin_lo
            sin_hi, cos_hi = 2.0 * sin_hi * cos_hi, 1.0 - 2.0 * sin_hi * sin_hi
        put(480, points)
        put(504, jnp.ones((8, lanes), F32))
        for i in range(SAMPLES):
            span = slice(i * lanes, (i + 1) * lanes)
            features = jnp.concatenate(
                [feats[b, pl.ds(i, ENC, stride=8), :] for b in range(blocks)], axis=1
            ).astype(BF16)
            enc[v, :, span] = features
            half = 0.5 * dot(w_in_t[v], features)
            act = (half + half * jnp.tanh(half)).astype(BF16)
            act_one[v, :, span] = act
            half = 0.5 * dot(w_hidden_t[v], act)
            act = (half + half * jnp.tanh(half)).astype(BF16)
            act_two[v, :, span] = act
            raw = dot(w_head_p[v], act)
            for c in range(4):
                raw_s[c, i, pl.ds(v, 1), :] = raw[c : c + 1]
            gap_s[i, pl.ds(v, 1), :] = gaps[i : i + 1]
        return carry

    lax.fori_loop(0, HELD, forward, 0)

    shade = [[sigmoid(raw_s[c, i]) for i in range(SAMPLES)] for c in range(3)]
    dense_slope, spans, share, clear = [], [], [], []
    depth = jnp.zeros((HELD, lanes), F32)
    through = jnp.ones((HELD, lanes), F32)
    color = [jnp.zeros((HELD, lanes), F32) for _ in range(3)]
    for i in range(SAMPLES):
        raw = raw_s[3, i]
        spacing = gap_s[i]
        tau = softplus(raw) * spacing
        depth = depth + tau
        share.append(through * (1.0 - jnp.exp(-tau)))
        through = jnp.exp(-depth)
        clear.append(through)
        dense_slope.append(sigmoid(raw))
        spans.append(spacing)
        color = [color[c] + share[i] * shade[c][i] for c in range(3)]

    turn[0:16, :] = jnp.concatenate(color + [through], axis=0)
    flipped = turn[...].T
    table_t[...] = flipped
    row_b = jnp.zeros((n_vol, 128), F32)
    for j in range(CAP):
        piece = table_t[pl.ds(j, n_vol, stride=CAP), :]
        row_b = row_b + (piece if j == 0 else pltpu.roll(piece, 16 * j, 1))
    send_b[...] = row_b.reshape(n_vol, 1, 128)
    recv_b[me_v] = send_b[me_v]
    exchange(send_b, recv_b, 1)

    def slopes(v, carry):
        for i in range(SAMPLES):
            span = slice(i * lanes, (i + 1) * lanes)
            for w_t, before_s, after_s, slope_s in (
                (w_in_t, enc, act_one, slope_one),
                (w_hidden_t, act_one, act_two, slope_two),
            ):
                pre = dot(w_t[v], before_s[v, :, span])
                gate = 0.5 + 0.5 * jnp.tanh(0.5 * pre)
                slope_s[v, :, span] = (gate + pre * gate * (1.0 - gate)).astype(BF16)
        return carry

    lax.fori_loop(0, HELD // 2, slopes, 0)
    await_all(recv_b, 3)

    owner_hot = one_hot(n_vol, owner).astype(BF16)
    arrived = recv_b[...].reshape(n_vol, 128)
    arrived = jnp.concatenate([arrived, jnp.zeros((128 - n_vol, 128), F32)], axis=0)
    arrived_t = arrived.T[:, 0:n_vol]
    found = dot(split3(arrived_t, 1), jnp.concatenate([owner_hot] * 3, axis=0))
    spot = lax.broadcasted_iota(jnp.int32, (128, segs), 0)
    mine = lax.bitwise_and(spot, 0x73) == rank * 16 + held
    found = jnp.where(mine, found, 0.0)
    total = found[0:16]
    for j in range(1, CAP):
        total = total + found[16 * j : 16 * j + 16]
    per_seg = [jnp.sum(total[4 * c : 4 * c + 4], axis=0, keepdims=True) for c in range(4)]
    carried = per_seg[3][:, :rays]
    behind = jnp.zeros((1, rays), F32)
    cots = []
    for c in range(3):
        near, far = per_seg[c][:, :rays], per_seg[c][:, rays:]
        value = near + carried * far
        out_color[c : c + 1, :] = value
        slope = (value - target[c : c + 1, :]) * (1.0 / n_rep)
        behind = behind + slope * far
        cots.append(jnp.concatenate([slope, carried * slope], axis=1))
    cots.append(jnp.concatenate([behind, jnp.zeros((1, rays), F32)], axis=1))
    cots = jnp.concatenate([jnp.broadcast_to(x, (4, segs)) for x in cots], axis=0)
    cots = jnp.where(mine, jnp.concatenate([cots] * CAP, axis=0), 0.0)
    row_c = dot_nt(owner_hot, split3(cots, 0))
    row_c = (row_c[:, 0:128] + row_c[:, 128:256]) + row_c[:, 256:384]
    send_c[...] = row_c.reshape(n_vol, 1, 128)
    recv_c[me_v] = send_c[me_v]
    exchange(send_c, recv_c, 2)

    lax.fori_loop(HELD // 2, HELD, slopes, 0)
    await_all(recv_c, 5)

    row_c = recv_c[...].reshape(n_vol, 128)
    for j in range(CAP):
        piece = row_c if j == 0 else pltpu.roll(row_c, 128 - 16 * j, 1)
        table_t[pl.ds(j, n_vol, stride=CAP), :] = piece
    cots = table_t[...].T[0:16]
    cot_color = [cots[4 * c : 4 * c + 4] for c in range(3)]
    later = through * cots[12:16]
    for i in reversed(range(SAMPLES)):
        pull = sum(cot_color[c] * shade[c][i] for c in range(3))
        cot_raw = [
            cot_color[c] * share[i] * (shade[c][i] * (1.0 - shade[c][i])) for c in range(3)
        ]
        cot_raw.append((clear[i] * pull - later) * spans[i] * dense_slope[i])
        later = later + share[i] * pull
        for c in range(4):
            for v in range(HELD):
                cot_f[v, c : c + 1, i * lanes : (i + 1) * lanes] = cot_raw[c][v : v + 1]

    def pair_copy(v):
        return pltpu.make_async_remote_copy(
            src_ref=part.at[v, 1 - me_c],
            dst_ref=pair_in.at[v],
            send_sem=pair_sem.at[0, v],
            recv_sem=pair_sem.at[1, v],
            device_id=(sibling, me_v),
            device_id_type=MESH,
        )

    def pass_on(v):
        pair_copy(v).wait()
        both = part[v, me_c] + pair_in[v]
        block_out[v] = both.astype(BF16)
        own_block[...] = both
        pair_in[v, 0] = own_block[me_y]
        block_in[v, me_y] = jnp.zeros((rows, PACK), BF16)

        def start(k, carry):
            y = lax.rem(me_y + k, n_y)
            pltpu.make_async_remote_copy(
                src_ref=block_out.at[v, y],
                dst_ref=block_in.at[v, me_y],
                send_sem=block_sem.at[0, v],
                recv_sem=block_sem.at[1, v],
                device_id=(y * 2 + me_c, me_v),
                device_id_type=MESH,
            ).start()
            return carry

        lax.fori_loop(1, n_y, start, 0)

    def backward(v, carry):
        for i in range(SAMPLES):
            span = slice(i * lanes, (i + 1) * lanes)
            cot_raw = cot_f[v, :, span].astype(BF16)
            cot = dot(w_head_t[v], cot_raw) * slope_two[v, :, span].astype(F32)
            cot = cot.astype(BF16)
            cot_two_s[:, span] = cot
            cot = dot(w_hidden[v], cot) * slope_one[v, :, span].astype(F32)
            cot_one_s[:, span] = cot.astype(BF16)
        d_mid = dot_nt(act_one[v], cot_two_s[...])
        d_first = dot_nt(cot_one_s[...], enc[v])
        d_last = dot_nt(act_two[v], cot_f[v].astype(BF16))
        side = jnp.concatenate([d_first, d_last, jnp.zeros((WIDTH, 48), F32)], axis=1)
        for r in range(n_rep):
            part[v, r % 2, r // 2, :, 0:WIDTH] = d_mid[r * rows : (r + 1) * rows]
            part[v, r % 2, r // 2, :, WIDTH:PACK] = side[r * rows : (r + 1) * rows]
        pair_copy(v).start()

        @pl.when(v > 0)
        def _():
            pass_on(v - 1)

        return carry

    lax.fori_loop(0, HELD, backward, 0)
    pass_on(HELD - 1)

    heads = []
    for v in range(HELD):
        span = block_in.at[v, pl.ds(0, n_y - 1)]
        pltpu.make_async_copy(span, span, block_sem.at[1, v]).wait()
        whole = pair_in[v, 0]
        for y in range(n_y):
            whole = whole + block_in[v, y].astype(F32)
        out_hidden[v] = whole[:, 0:WIDTH]
        out_in[v] = whole[:, WIDTH : WIDTH + ENC]
        heads.append(whole[:, WIDTH:PACK])
    heads.append(jnp.zeros((max(128 - HELD * rows, 0), 128), F32))
    heads = jnp.concatenate(heads, axis=0).T
    for v in range(HELD):
        out_head[v] = heads[ENC : ENC + 4, v * rows : (v + 1) * rows]

    for number, buffer in ((0, send_a), (1, send_b), (2, send_c)):
        await_all(buffer, 2 * number)
    for v in range(HELD):
        span = block_out.at[v, pl.ds(0, n_y - 1)]
        pltpu.make_async_copy(span, span, block_sem.at[0, v]).wait()


def solution(mesh):
    n_rep, n_vol = mesh.shape["rep"], mesh.shape["vol"]

    def local(positions, spacing, volume_ids, target, w_in, w_hidden, w_head):
        rays = volume_ids.shape[0]
        lanes = n_vol * CAP
        wide = SAMPLES * lanes
        rows = WIDTH // n_rep
        n_y = n_rep // 2
        vmem = pl.BlockSpec(memory_space=pltpu.VMEM)
        outs = pl.pallas_call(
            functools.partial(kernel, n_rep, n_vol, rays),
            out_shape=(
                jax.ShapeDtypeStruct((3, rays), F32),
                jax.ShapeDtypeStruct((HELD, rows, ENC), F32),
                jax.ShapeDtypeStruct((HELD, rows, WIDTH), F32),
                jax.ShapeDtypeStruct((HELD, 4, rows), F32),
            ),
            in_specs=[vmem] * 7,
            out_specs=[vmem] * 4,
            scratch_shapes=[
                pltpu.VMEM((n_vol, CAP, 128), F32),
                pltpu.VMEM((n_vol, CAP, 128), F32),
                pltpu.VMEM((n_vol, 1, 128), F32),
                pltpu.VMEM((n_vol, 1, 128), F32),
                pltpu.VMEM((n_vol, 1, 128), F32),
                pltpu.VMEM((n_vol, 1, 128), F32),
                pltpu.VMEM((128, lanes), F32),
                pltpu.VMEM((pl.cdiv(lanes, 128), ENC * 8, min(lanes, 128)), F32),
                pltpu.VMEM((HELD, ENC, wide), BF16),
                pltpu.VMEM((HELD, WIDTH, wide), BF16),
                pltpu.VMEM((HELD, WIDTH, wide), BF16),
                pltpu.VMEM((HELD, WIDTH, wide), BF16),
                pltpu.VMEM((HELD, WIDTH, wide), BF16),
                pltpu.VMEM((4, SAMPLES, HELD, lanes), F32),
                pltpu.VMEM((SAMPLES, HELD, lanes), F32),
                pltpu.VMEM((HELD, 16, wide), F32),
                pltpu.VMEM((WIDTH, wide), BF16),
                pltpu.VMEM((WIDTH, wide), BF16),
                pltpu.VMEM((128, lanes), F32),
                pltpu.VMEM((lanes, 128), F32),
                pltpu.VMEM((HELD, WIDTH, ENC), BF16),
                pltpu.VMEM((HELD, WIDTH, WIDTH), BF16),
                pltpu.VMEM((HELD, 16, WIDTH), BF16),
                pltpu.VMEM((HELD, WIDTH, 16), BF16),
                pltpu.VMEM((HELD, 2, n_y, rows, PACK), F32),
                pltpu.VMEM((HELD, n_y, rows, PACK), F32),
                pltpu.VMEM((HELD, n_y, rows, PACK), BF16),
                pltpu.VMEM((HELD, n_y, rows, PACK), BF16),
                pltpu.VMEM((n_y, rows, PACK), F32),
                pltpu.SemaphoreType.DMA((6,)),
                pltpu.SemaphoreType.DMA((2, HELD)),
                pltpu.SemaphoreType.DMA((2, HELD)),
            ],
            compiler_params=pltpu.CompilerParams(
                collective_id=0, has_side_effects=True, vmem_limit_bytes=56 * 1024 * 1024
            ),
        )(
            jnp.transpose(positions, (1, 2, 0)),
            jnp.transpose(spacing, (1, 2, 0)),
            volume_ids.T,
            target,
            w_in,
            w_hidden,
            w_head,
        )
        color, grad_in, grad_hidden, grad_head = outs
        return color, jnp.swapaxes(grad_in, 1, 2), grad_hidden, grad_head

    return jax.shard_map(
        local,
        mesh=mesh,
        in_specs=(
            P(("rep", "vol"), None, None),
            P(("rep", "vol"), None, None),
            P(("rep", "vol"), None),
            P(None, ("rep", "vol")),
            P("vol", None, None),
            P("vol", None, None),
            P("vol", None, None),
        ),
        out_specs=(
            P(None, ("rep", "vol")),
            P("vol", None, "rep"),
            P("vol", "rep", None),
            P("vol", None, "rep"),
        ),
        check_vma=False,
    )
```

time: 394 us -> 70.6 us (0.18)
  waiting for transfers between devices: 218 us -> 0 us
  Pallas kernels: 0 us -> 65.7 us
  other arithmetic: 54.9 us -> 0 us
  matrix products: 42.7 us -> 0 us
  starting transfers between devices: 32.4 us -> 0 us
  local copies, waits for them, and re-layouts: 28.9 us -> 3.97 us
  between operations: 14.3 us -> 0.65 us
    reduce_scatter x2 -> x0, waiting for transfers between devices: 122 us -> none  [the longest x1 62 us: local(): lax.psum_scatter(partial_grads[1], 'rep', scatter_dimension=1, tiled=True)]
    pallas_call x0 -> x1, Pallas kernels: none -> 65.7 us  [local(): pl.pallas_call(functools.partial(kernel, n_rep, n_vol, rays), out_shape=(...]
    unnamed x4 -> x0, waiting for transfers between devices: 53.9 us -> none
    dot_general x36 -> x0, matrix products: 42.7 us -> none  [product(): return jnp.dot(left, right, preferred_element_type=jnp.float32)]
    another operation x7 -> x0, other arithmetic: 42.7 us -> none  [the longest x2 40.6 us: segment_values(): before = jnp.cumsum(tau, axis=-1) - tau]
    all_to_all x4 -> x0, waiting for transfers between devices: 42.5 us -> none  [the longest x1 24.2 us: local(): lax.all_to_all(outgoing, 'vol', split_axis=0, concat_axis=0, tiled=True)]
    all_to_all x4 -> x0, starting transfers between devices: 32.1 us -> none  [the longest x1 13.7 us: local(): lax.all_to_all(gap_slots.astype(jnp.bfloat16), 'vol', split_axis=0, conca...]
    scatter x4 -> x0, local copies, waits for them, and re-layouts: 7.26 us -> none  [the longest x1 3.49 us: local(): jnp.zeros((volume_count * capacity, sample_count * ENC), jnp.bfloat16)]
  transfers between devices with their start and end apart: 7 -> 0, of which waited for: 7 -> 0; matrix products, arithmetic and copies ran while one was open for 3% -> 0% of each run, Pallas kernels for 0% -> 0%
where the time goes in v1:
time: 70.6 us; the launch traced here: 70.4 us
  Pallas kernels  65.7 us (93%)
  local copies, waits for them, and re-layouts  3.97 us (6%)
    pallas_call x1, Pallas kernels, local(): pl.pallas_call(functools.partial(kernel, n_rep, n_vol, rays), out_shape=(...  65.7 us
    unnamed x8, local copies, waits for them, and re-layouts  3.97 us

profile of v1, /device:TPU:1, one launch (start us, length us, event | category | flops | bytes accessed | tf_op | source)
XLA Modules:
  0.0 70.4 jit_solution(3271528385871054322)
XLA Ops:
  0.6 65.7 %shard_map.102 = (f32[3,256]{1,0:T(4,128)}, f32[4,16,64]{2,1,0:T(8,128)}, f32[4,16,256]{2,1,0:T(8,128)}, f32[4,4,16]{2,1,0:T(4,128)}) custom-call(f32[2,24,256]{2,1,0:T(8,128)} %bitcast.4, f32[2,8,256]{2,1,0:T(8,128)} %bitcast.6, s32[2,256]{1,0:T(2,128)} %bitcast.7, f32[3,256]{1,0:T(4,128)} %target.1, bf16[4,64,256]{2,1,0:T(8,128)(2,1)} %w_in.1, ...), custom_call_target="tpu_custom_call" | custom-call | tf_op jit(solution)/shard_map/pallas_call | solution.py:413
  66.4 0.0 copy-start
  66.4 1.3 %copy.15 = f32[3,256]{1,0:T(4,128)} copy(f32[3,256]{1,0:T(4,128)} %get-tuple-element.16) | data formatting | bytes 6144
  67.7 1.4 %copy.16 = f32[4,64,16]{1,2,0:T(8,128)} copy(f32[4,64,16]{1,2,0:T(8,128)} %bitcast.5) | data formatting | bytes 32768
  69.1 0.0 copy-done
  69.1 0.0 copy-start.1
  69.1 0.6 copy.17
  69.7 0.1 copy-done.1
  69.8 0.6 copy.18
Async XLA Ops:
  66.4 2.7 %copy-start = (f32[4,16,256]{2,1,0:T(8,128)S(1)}, f32[4,16,256]{2,1,0:T(8,128)}, u32[]{:S(2)}) copy-start(f32[4,16,256]{2,1,0:T(8,128)} %get-tuple-element.18) | copy-start | bytes 196612
  69.1 0.7 copy-start.1

commit v2 on v1

--- a/solution.py
+++ b/solution.py
@@ -68,14 +68,15 @@
 
 def kernel(
     n_rep, n_vol, rays,
-    pos, gap, ids, target, w_in, w_hidden, w_head,
+    pos_h, gap_h, ids_h, target_h, w_in_h, w_hidden_h, w_head_h,
     out_color, out_in, out_hidden, out_head,
     send_a, recv_a, send_b, recv_b, send_c, recv_c,
     table, feats, enc, act_one, act_two, slope_one, slope_two,
     raw_s, gap_s, cot_f, cot_two_s, cot_one_s, turn, table_t,
-    w_in_t, w_hidden_t, w_head_p, w_head_t,
+    w_in_t, w_hidden_t, w_head_p, w_head_w,
     part, pair_in, block_out, block_in, own_block,
-    sem, pair_sem, block_sem,
+    pos, gap, ids, target, w_in, w_hidden, w_head,
+    sem, pair_sem, block_sem, load_sem,
 ):
     me_r, me_v = lax.axis_index("rep"), lax.axis_index("vol")
     n_y = n_rep // 2
@@ -85,14 +86,33 @@
     volumes = n_vol * HELD
     rows = WIDTH // n_rep
 
+    n_z, n_x = n_vol // 4, 4
+    me_z, me_x = me_v // n_x, lax.rem(me_v, n_x)
+
+    def far_first(k, n):
+        half = (k + 1) // 2
+        return n // 2 + jnp.where(lax.rem(k, 2) == 0, half, -half)
+
     def vol_peer(k):
-        return lax.rem(me_v + k, n_vol)
-
-    def rep_peer(k):
-        return lax.rem(me_y + k, n_y) * 2 + me_c
+        z = lax.rem(me_z + far_first(k // n_x, n_z), n_z)
+        x = lax.rem(me_x + far_first(lax.rem(k, n_x), n_x), n_x)
+        return z * n_x + x
+
+    def y_peer(k):
+        return lax.rem(me_y + far_first(k, n_y), n_y)
 
     sibling = me_y * 2 + 1 - me_c
-
+    blocks, block = feats.shape[0], feats.shape[2]
+
+    loads = [
+        pltpu.make_async_copy(source, place, load_sem.at[number])
+        for number, (source, place) in enumerate(
+            (
+                (ids_h, ids), (pos_h, pos), (gap_h, gap), (w_in_h, w_in),
+                (w_hidden_h, w_hidden), (w_head_h, w_head), (target_h, target),
+            )
+        )
+    ]
     barrier = pltpu.get_barrier_semaphore()
 
     def greet_vol(k, carry):
@@ -100,12 +120,16 @@
         return carry
 
     def greet_rep(k, carry):
-        pl.semaphore_signal(barrier, inc=1, device_id=(rep_peer(k), me_v), device_id_type=MESH)
+        pl.semaphore_signal(barrier, inc=1, device_id=(y_peer(k) * 2 + me_c, me_v), device_id_type=MESH)
         return carry
 
-    lax.fori_loop(1, n_vol, greet_vol, 0)
-    lax.fori_loop(1, n_y, greet_rep, 0)
+    lax.fori_loop(0, n_vol - 1, greet_vol, 0)
+    lax.fori_loop(0, n_y - 1, greet_rep, 0)
     pl.semaphore_signal(barrier, inc=1, device_id=(sibling, me_v), device_id_type=MESH)
+
+    for load in loads:
+        load.start()
+    loads[0].wait()
 
     id_row = jnp.concatenate([ids[0:1, :], ids[1:2, :]], axis=1)
     hot = one_hot(volumes, id_row)
@@ -128,6 +152,8 @@
     owner = lax.shift_right_logical(id_row, 2)
     held = lax.bitwise_and(id_row, 3)
     place_hot = one_hot(lanes, owner * CAP + rank).astype(BF16)
+    loads[1].wait()
+    loads[2].wait()
     vals = jnp.concatenate(
         [
             jnp.concatenate([pos[0], gap[0]], axis=0),
@@ -155,7 +181,7 @@
             ).start()
             return carry
 
-        lax.fori_loop(1, n_vol, start, 0)
+        lax.fori_loop(0, n_vol - 1, start, 0)
 
     def await_all(buffer, which):
         span = buffer.at[pl.ds(0, n_vol - 1)]
@@ -166,21 +192,24 @@
     cot_f[...] = jnp.zeros_like(cot_f)
     turn[...] = jnp.zeros_like(turn)
     w_head_p[...] = jnp.zeros_like(w_head_p)
+
+    for load in loads[3:]:
+        load.wait()
 
     def turn_weights(v, carry):
         w_in_t[v] = w_in[v].astype(F32).T.astype(BF16)
         w_hidden_t[v] = w_hidden[v].astype(F32).T.astype(BF16)
         head = jnp.concatenate([w_head[v].astype(F32), jnp.zeros((124, WIDTH), F32)], axis=0)
         w_head_p[v] = head[0:16].astype(BF16)
-        w_head_t[v] = head.T[:, 0:16].astype(BF16)
+        head_t = head.T
+        for c in range(4):
+            w_head_w[v, c] = jnp.broadcast_to(head_t[:, c : c + 1], (WIDTH, block))
         return carry
 
     lax.fori_loop(0, HELD, turn_weights, 0)
 
     await_all(recv_a, 1)
     table[...] = recv_a[...].reshape(lanes, 128).T
-
-    blocks, block = feats.shape[0], feats.shape[2]
 
     def put(at, values):
         for b in range(blocks):
@@ -216,10 +245,11 @@
             half = 0.5 * dot(w_hidden_t[v], act)
             act = (half + half * jnp.tanh(half)).astype(BF16)
             act_two[v, :, span] = act
-            raw = dot(w_head_p[v], act)
+            gap_s[i, pl.ds(v, 1), :] = gaps[i : i + 1]
+        for i in range(SAMPLES):
+            raw = dot(w_head_p[v], act_two[v, :, i * lanes : (i + 1) * lanes])
             for c in range(4):
                 raw_s[c, i, pl.ds(v, 1), :] = raw[c : c + 1]
-            gap_s[i, pl.ds(v, 1), :] = gaps[i : i + 1]
         return carry
 
     lax.fori_loop(0, HELD, forward, 0)
@@ -261,7 +291,7 @@
             ):
                 pre = dot(w_t[v], before_s[v, :, span])
                 gate = 0.5 + 0.5 * jnp.tanh(0.5 * pre)
-                slope_s[v, :, span] = (gate + pre * gate * (1.0 - gate)).astype(BF16)
+                slope_s[v, :, span] = gate + pre * gate * (1.0 - gate)
         return carry
 
     lax.fori_loop(0, HELD // 2, slopes, 0)
@@ -338,7 +368,7 @@
         block_in[v, me_y] = jnp.zeros((rows, PACK), BF16)
 
         def start(k, carry):
-            y = lax.rem(me_y + k, n_y)
+            y = y_peer(k)
             pltpu.make_async_remote_copy(
                 src_ref=block_out.at[v, y],
                 dst_ref=block_in.at[v, me_y],
@@ -349,21 +379,26 @@
             ).start()
             return carry
 
-        lax.fori_loop(1, n_y, start, 0)
+        lax.fori_loop(0, n_y - 1, start, 0)
 
     def backward(v, carry):
         for i in range(SAMPLES):
             span = slice(i * lanes, (i + 1) * lanes)
-            cot_raw = cot_f[v, :, span].astype(BF16)
-            cot = dot(w_head_t[v], cot_raw) * slope_two[v, :, span].astype(F32)
+            cot_raw = cot_f[v, 0:4, span].astype(BF16).astype(F32)
+            cot = sum(
+                cot_raw[c : c + 1] * jnp.concatenate([w_head_w[v, c]] * blocks, axis=1)
+                for c in range(4)
+            )
+            cot = cot * slope_two[v, :, span]
             cot = cot.astype(BF16)
             cot_two_s[:, span] = cot
-            cot = dot(w_hidden[v], cot) * slope_one[v, :, span].astype(F32)
+            cot = dot(w_hidden[v], cot) * slope_one[v, :, span]
             cot_one_s[:, span] = cot.astype(BF16)
         d_mid = dot_nt(act_one[v], cot_two_s[...])
         d_first = dot_nt(cot_one_s[...], enc[v])
-        d_last = dot_nt(act_two[v], cot_f[v].astype(BF16))
-        side = jnp.concatenate([d_first, d_last, jnp.zeros((WIDTH, 48), F32)], axis=1)
+        d_last = dot_nt(cot_f[v].astype(BF16), act_two[v])
+        d_last = jnp.concatenate([d_last, jnp.zeros((112, WIDTH), F32)], axis=0).T[:, 0:64]
+        side = jnp.concatenate([d_first, d_last], axis=1)
         for r in range(n_rep):
             part[v, r % 2, r // 2, :, 0:WIDTH] = d_mid[r * rows : (r + 1) * rows]
             part[v, r % 2, r // 2, :, WIDTH:PACK] = side[r * rows : (r + 1) * rows]
@@ -400,6 +435,11 @@
         pltpu.make_async_copy(span, span, block_sem.at[0, v]).wait()
 
 
+def hand_over(*refs):
+    for source, result in zip(refs[:4], refs[4:]):
+        result[...] = source[...]
+
+
 def solution(mesh):
     n_rep, n_vol = mesh.shape["rep"], mesh.shape["vol"]
 
@@ -410,15 +450,16 @@
         rows = WIDTH // n_rep
         n_y = n_rep // 2
         vmem = pl.BlockSpec(memory_space=pltpu.VMEM)
+        shapes = (
+            jax.ShapeDtypeStruct((3, rays), F32),
+            jax.ShapeDtypeStruct((HELD, rows, ENC), F32),
+            jax.ShapeDtypeStruct((HELD, rows, WIDTH), F32),
+            jax.ShapeDtypeStruct((HELD, 4, rows), F32),
+        )
         outs = pl.pallas_call(
             functools.partial(kernel, n_rep, n_vol, rays),
-            out_shape=(
-                jax.ShapeDtypeStruct((3, rays), F32),
-                jax.ShapeDtypeStruct((HELD, rows, ENC), F32),
-                jax.ShapeDtypeStruct((HELD, rows, WIDTH), F32),
-                jax.ShapeDtypeStruct((HELD, 4, rows), F32),
-            ),
-            in_specs=[vmem] * 7,
+            out_shape=shapes,
+            in_specs=[pl.BlockSpec(memory_space=pl.ANY)] * 7,
             out_specs=[vmem] * 4,
             scratch_shapes=[
                 pltpu.VMEM((n_vol, CAP, 128), F32),
@@ -432,8 +473,8 @@
                 pltpu.VMEM((HELD, ENC, wide), BF16),
                 pltpu.VMEM((HELD, WIDTH, wide), BF16),
                 pltpu.VMEM((HELD, WIDTH, wide), BF16),
-                pltpu.VMEM((HELD, WIDTH, wide), BF16),
-                pltpu.VMEM((HELD, WIDTH, wide), BF16),
+                pltpu.VMEM((HELD, WIDTH, wide), F32),
+                pltpu.VMEM((HELD, WIDTH, wide), F32),
                 pltpu.VMEM((4, SAMPLES, HELD, lanes), F32),
                 pltpu.VMEM((SAMPLES, HELD, lanes), F32),
                 pltpu.VMEM((HELD, 16, wide), F32),
@@ -444,15 +485,23 @@
                 pltpu.VMEM((HELD, WIDTH, ENC), BF16),
                 pltpu.VMEM((HELD, WIDTH, WIDTH), BF16),
                 pltpu.VMEM((HELD, 16, WIDTH), BF16),
-                pltpu.VMEM((HELD, WIDTH, 16), BF16),
+                pltpu.VMEM((HELD, 4, WIDTH, min(lanes, 128)), F32),
                 pltpu.VMEM((HELD, 2, n_y, rows, PACK), F32),
                 pltpu.VMEM((HELD, n_y, rows, PACK), F32),
                 pltpu.VMEM((HELD, n_y, rows, PACK), BF16),
                 pltpu.VMEM((HELD, n_y, rows, PACK), BF16),
                 pltpu.VMEM((n_y, rows, PACK), F32),
+                pltpu.VMEM((2, 3 * SAMPLES, rays), F32),
+                pltpu.VMEM((2, SAMPLES, rays), F32),
+                pltpu.VMEM((2, rays), jnp.int32),
+                pltpu.VMEM((3, rays), F32),
+                pltpu.VMEM(w_in.shape, BF16),
+                pltpu.VMEM(w_hidden.shape, BF16),
+                pltpu.VMEM(w_head.shape, BF16),
                 pltpu.SemaphoreType.DMA((6,)),
                 pltpu.SemaphoreType.DMA((2, HELD)),
                 pltpu.SemaphoreType.DMA((2, HELD)),
+                pltpu.SemaphoreType.DMA((7,)),
             ],
             compiler_params=pltpu.CompilerParams(
                 collective_id=0, has_side_effects=True, vmem_limit_bytes=56 * 1024 * 1024
@@ -466,7 +515,9 @@
             w_hidden,
             w_head,
         )
-        color, grad_in, grad_hidden, grad_head = outs
+        color, grad_in, grad_hidden, grad_head = pl.pallas_call(
+            hand_over, out_shape=shapes, in_specs=[vmem] * 4, out_specs=[vmem] * 4
+        )(*outs)
         return color, jnp.swapaxes(grad_in, 1, 2), grad_hidden, grad_head
 
     return jax.shard_map(

time: 70.6 us -> 58.1 us (0.82)
  Pallas kernels: 65.7 us -> 57.3 us
  local copies, waits for them, and re-layouts: 3.97 us -> 0 us
    pallas_call x1 -> x2, Pallas kernels: 65.7 us -> 57.3 us  [the longest x1 55.8 us: local(): pl.pallas_call(functools.partial(kernel, n_rep, n_vol, rays), out_shape=s...]
    unnamed x8 -> x0, local copies, waits for them, and re-layouts: 3.97 us -> none
where the time goes in v2:
time: 58.1 us; the launch traced here: 57.9 us
  Pallas kernels  57.3 us (99%)
  between operations  0.64 us (1%)
    pallas_call x1, Pallas kernels, local(): pl.pallas_call(functools.partial(kernel, n_rep, n_vol, rays), out_shape=s...  55.8 us
    pallas_call x1, Pallas kernels, local(): pl.pallas_call(hand_over, out_shape=shapes, in_specs=[vmem] * 4, out_spec...  1.52 us

profile of v2, /device:TPU:1, one launch (start us, length us, event | category | flops | bytes accessed | tf_op | source)
XLA Modules:
  0.0 57.9 jit_solution(15544645523919249183)
XLA Ops:
  0.6 55.8 %shard_map.102 = (f32[3,256]{1,0:T(4,128)}, f32[4,16,64]{2,1,0:T(8,128)}, f32[4,16,256]{2,1,0:T(8,128)}, f32[4,4,16]{2,1,0:T(4,128)}) custom-call(f32[2,24,256]{2,1,0:T(8,128)} %bitcast.4, f32[2,8,256]{2,1,0:T(8,128)} %bitcast.5, s32[2,256]{1,0:T(2,128)} %bitcast.6, f32[3,256]{1,0:T(4,128)} %target_h.1, bf16[4,64,256]{2,1,0:T(8,128)(2,1)} %w_in_h.1, ...), custom_call_target="tpu_custom_call" | custom-call | tf_op jit(solution)/shard_map/pallas_call | solution.py:459
  56.4 1.5 %shard_map.103 = (f32[3,256]{1,0:T(4,128)}, f32[4,16,64]{2,1,0:T(8,128)}, f32[4,16,256]{2,1,0:T(8,128)}, f32[4,4,16]{2,1,0:T(4,128)}) custom-call(f32[3,256]{1,0:T(4,128)} %get-tuple-element.12.refs_0_, f32[4,16,64]{2,1,0:T(8,128)} %get-tuple-element.13.refs_1_, f32[4,16,256]{2,1,0:T(8,128)} %get-tuple-element.14.refs_2_, f32[4,4,16]{2,1,0:T(4,128)} %get-tuple-element.15.refs_3_), custom_call_target="tpu_custom_call" | custom-call | tf_op jit(solution)/shard_map/pallas_call | solution.py:518

commit v3 on v2

--- a/solution.py
+++ b/solution.py
@@ -72,7 +72,7 @@
     out_color, out_in, out_hidden, out_head,
     send_a, recv_a, send_b, recv_b, send_c, recv_c,
     table, feats, enc, act_one, act_two, slope_one, slope_two,
-    raw_s, gap_s, cot_f, cot_two_s, cot_one_s, turn, table_t,
+    mine_s, raw_s, gap_s, cot_f, cot_two_s, cot_one_s, turn, table_t,
     w_in_t, w_hidden_t, w_head_p, w_head_w,
     part, pair_in, block_out, block_in, own_block,
     pos, gap, ids, target, w_in, w_hidden, w_head,
@@ -86,21 +86,16 @@
     volumes = n_vol * HELD
     rows = WIDTH // n_rep
 
-    n_z, n_x = n_vol // 4, 4
-    me_z, me_x = me_v // n_x, lax.rem(me_v, n_x)
-
-    def far_first(k, n):
-        half = (k + 1) // 2
-        return n // 2 + jnp.where(lax.rem(k, 2) == 0, half, -half)
-
-    def vol_peer(k):
-        z = lax.rem(me_z + far_first(k // n_x, n_z), n_z)
-        x = lax.rem(me_x + far_first(lax.rem(k, n_x), n_x), n_x)
-        return z * n_x + x
-
-    def y_peer(k):
-        return lax.rem(me_y + far_first(k, n_y), n_y)
-
+    n_x = min(4, n_vol)
+    n_z = n_vol // n_x
+
+    def far_first(n):
+        return sorted(range(n), key=lambda step: -min(step, n - step))
+
+    zs = [lax.rem(me_v // n_x + step, n_z) * n_x for step in far_first(n_z)]
+    xs = [lax.rem(lax.rem(me_v, n_x) + step, n_x) for step in far_first(n_x)]
+    vol_peers = [z + x for z in zs for x in xs][:-1]
+    y_peers = [lax.rem(me_y + step, n_y) for step in far_first(n_y)][:-1]
     sibling = me_y * 2 + 1 - me_c
     blocks, block = feats.shape[0], feats.shape[2]
 
@@ -115,16 +110,10 @@
     ]
     barrier = pltpu.get_barrier_semaphore()
 
-    def greet_vol(k, carry):
-        pl.semaphore_signal(barrier, inc=1, device_id=(me_r, vol_peer(k)), device_id_type=MESH)
-        return carry
-
-    def greet_rep(k, carry):
-        pl.semaphore_signal(barrier, inc=1, device_id=(y_peer(k) * 2 + me_c, me_v), device_id_type=MESH)
-        return carry
-
-    lax.fori_loop(0, n_vol - 1, greet_vol, 0)
-    lax.fori_loop(0, n_y - 1, greet_rep, 0)
+    for peer in vol_peers:
+        pl.semaphore_signal(barrier, inc=1, device_id=(me_r, peer), device_id_type=MESH)
+    for peer in y_peers:
+        pl.semaphore_signal(barrier, inc=1, device_id=(peer * 2 + me_c, me_v), device_id_type=MESH)
     pl.semaphore_signal(barrier, inc=1, device_id=(sibling, me_v), device_id_type=MESH)
 
     for load in loads:
@@ -169,8 +158,7 @@
     pl.semaphore_wait(barrier, n_vol - 1 + n_y)
 
     def exchange(source, landing, number):
-        def start(k, carry):
-            peer = vol_peer(k)
+        for peer in vol_peers:
             pltpu.make_async_remote_copy(
                 src_ref=source.at[peer],
                 dst_ref=landing.at[me_v],
@@ -179,9 +167,6 @@
                 device_id=(me_r, peer),
                 device_id_type=MESH,
             ).start()
-            return carry
-
-        lax.fori_loop(0, n_vol - 1, start, 0)
 
     def await_all(buffer, which):
         span = buffer.at[pl.ds(0, n_vol - 1)]
@@ -294,17 +279,19 @@
                 slope_s[v, :, span] = gate + pre * gate * (1.0 - gate)
         return carry
 
+    owner_hot = one_hot(n_vol, owner).astype(BF16)
+    spot = lax.broadcasted_iota(jnp.int32, (128, segs), 0)
+    mine = jnp.where(lax.bitwise_and(spot, 0x73) == rank * 16 + held, 1.0, 0.0)
+    mine_s[...] = mine
     lax.fori_loop(0, HELD // 2, slopes, 0)
     await_all(recv_b, 3)
 
-    owner_hot = one_hot(n_vol, owner).astype(BF16)
+    mine = mine_s[...]
     arrived = recv_b[...].reshape(n_vol, 128)
     arrived = jnp.concatenate([arrived, jnp.zeros((128 - n_vol, 128), F32)], axis=0)
     arrived_t = arrived.T[:, 0:n_vol]
     found = dot(split3(arrived_t, 1), jnp.concatenate([owner_hot] * 3, axis=0))
-    spot = lax.broadcasted_iota(jnp.int32, (128, segs), 0)
-    mine = lax.bitwise_and(spot, 0x73) == rank * 16 + held
-    found = jnp.where(mine, found, 0.0)
+    found = found * mine
     total = found[0:16]
     for j in range(1, CAP):
         total = total + found[16 * j : 16 * j + 16]
@@ -321,7 +308,7 @@
         cots.append(jnp.concatenate([slope, carried * slope], axis=1))
     cots.append(jnp.concatenate([behind, jnp.zeros((1, rays), F32)], axis=1))
     cots = jnp.concatenate([jnp.broadcast_to(x, (4, segs)) for x in cots], axis=0)
-    cots = jnp.where(mine, jnp.concatenate([cots] * CAP, axis=0), 0.0)
+    cots = jnp.concatenate([cots] * CAP, axis=0) * mine
     row_c = dot_nt(owner_hot, split3(cots, 0))
     row_c = (row_c[:, 0:128] + row_c[:, 128:256]) + row_c[:, 256:384]
     send_c[...] = row_c.reshape(n_vol, 1, 128)
@@ -367,8 +354,7 @@
         pair_in[v, 0] = own_block[me_y]
         block_in[v, me_y] = jnp.zeros((rows, PACK), BF16)
 
-        def start(k, carry):
-            y = y_peer(k)
+        for y in y_peers:
             pltpu.make_async_remote_copy(
                 src_ref=block_out.at[v, y],
                 dst_ref=block_in.at[v, me_y],
@@ -377,9 +363,6 @@
                 device_id=(y * 2 + me_c, me_v),
                 device_id_type=MESH,
             ).start()
-            return carry
-
-        lax.fori_loop(0, n_y - 1, start, 0)
 
     def backward(v, carry):
         for i in range(SAMPLES):
@@ -475,6 +458,7 @@
                 pltpu.VMEM((HELD, WIDTH, wide), BF16),
                 pltpu.VMEM((HELD, WIDTH, wide), F32),
                 pltpu.VMEM((HELD, WIDTH, wide), F32),
+                pltpu.VMEM((128, 2 * rays), F32),
                 pltpu.VMEM((4, SAMPLES, HELD, lanes), F32),
                 pltpu.VMEM((SAMPLES, HELD, lanes), F32),
                 pltpu.VMEM((HELD, 16, wide), F32),

time: 58.1 us -> 57.3 us (0.986)
  Pallas kernels: 57.3 us -> 56.5 us
    pallas_call x1, Pallas kernels: 55.8 us -> 55 us  [local(): pl.pallas_call(functools.partial(kernel, n_rep, n_vol, rays), out_shape=s...]
where the time goes in v3:
time: 57.3 us; the launch traced here: 57.1 us
  Pallas kernels  56.5 us (99%)
  between operations  0.64 us (1%)
    pallas_call x1, Pallas kernels, local(): pl.pallas_call(functools.partial(kernel, n_rep, n_vol, rays), out_shape=s...  55 us
    pallas_call x1, Pallas kernels, local(): pl.pallas_call(hand_over, out_shape=shapes, in_specs=[vmem] * 4, out_spec...  1.52 us

profile of v3, /device:TPU:1, one launch (start us, length us, event | category | flops | bytes accessed | tf_op | source)
XLA Modules:
  0.0 57.1 jit_solution(18299329161022956636)
XLA Ops:
  0.6 55.0 %shard_map.102 = (f32[3,256]{1,0:T(4,128)}, f32[4,16,64]{2,1,0:T(8,128)}, f32[4,16,256]{2,1,0:T(8,128)}, f32[4,4,16]{2,1,0:T(4,128)}) custom-call(f32[2,24,256]{2,1,0:T(8,128)} %bitcast.4, f32[2,8,256]{2,1,0:T(8,128)} %bitcast.5, s32[2,256]{1,0:T(2,128)} %bitcast.6, f32[3,256]{1,0:T(4,128)} %target_h.1, bf16[4,64,256]{2,1,0:T(8,128)(2,1)} %w_in_h.1, ...), custom_call_target="tpu_custom_call" | custom-call | tf_op jit(solution)/shard_map/pallas_call | solution.py:442
  55.6 1.5 %shard_map.103 = (f32[3,256]{1,0:T(4,128)}, f32[4,16,64]{2,1,0:T(8,128)}, f32[4,16,256]{2,1,0:T(8,128)}, f32[4,4,16]{2,1,0:T(4,128)}) custom-call(f32[3,256]{1,0:T(4,128)} %get-tuple-element.12.refs_0_, f32[4,16,64]{2,1,0:T(8,128)} %get-tuple-element.13.refs_1_, f32[4,16,256]{2,1,0:T(8,128)} %get-tuple-element.14.refs_2_, f32[4,4,16]{2,1,0:T(4,128)} %get-tuple-element.15.refs_3_), custom_call_target="tpu_custom_call" | custom-call | tf_op jit(solution)/shard_map/pallas_call | solution.py:502

commit v4 on v3

--- a/solution.py
+++ b/solution.py
@@ -182,8 +182,8 @@
         load.wait()
 
     def turn_weights(v, carry):
-        w_in_t[v] = w_in[v].astype(F32).T.astype(BF16)
-        w_hidden_t[v] = w_hidden[v].astype(F32).T.astype(BF16)
+        w_in_t[v] = (0.5 * w_in[v].astype(F32).T).astype(BF16)
+        w_hidden_t[v] = (0.5 * w_hidden[v].astype(F32).T).astype(BF16)
         head = jnp.concatenate([w_head[v].astype(F32), jnp.zeros((124, WIDTH), F32)], axis=0)
         w_head_p[v] = head[0:16].astype(BF16)
         head_t = head.T
@@ -224,10 +224,10 @@
                 [feats[b, pl.ds(i, ENC, stride=8), :] for b in range(blocks)], axis=1
             ).astype(BF16)
             enc[v, :, span] = features
-            half = 0.5 * dot(w_in_t[v], features)
+            half = dot(w_in_t[v], features)
             act = (half + half * jnp.tanh(half)).astype(BF16)
             act_one[v, :, span] = act
-            half = 0.5 * dot(w_hidden_t[v], act)
+            half = dot(w_hidden_t[v], act)
             act = (half + half * jnp.tanh(half)).astype(BF16)
             act_two[v, :, span] = act
             gap_s[i, pl.ds(v, 1), :] = gaps[i : i + 1]
@@ -240,7 +240,7 @@
     lax.fori_loop(0, HELD, forward, 0)
 
     shade = [[sigmoid(raw_s[c, i]) for i in range(SAMPLES)] for c in range(3)]
-    dense_slope, spans, share, clear = [], [], [], []
+    spans, share, clear = [], [], []
     depth = jnp.zeros((HELD, lanes), F32)
     through = jnp.ones((HELD, lanes), F32)
     color = [jnp.zeros((HELD, lanes), F32) for _ in range(3)]
@@ -252,7 +252,6 @@
         share.append(through * (1.0 - jnp.exp(-tau)))
         through = jnp.exp(-depth)
         clear.append(through)
-        dense_slope.append(sigmoid(raw))
         spans.append(spacing)
         color = [color[c] + share[i] * shade[c][i] for c in range(3)]
 
@@ -267,6 +266,11 @@
     recv_b[me_v] = send_b[me_v]
     exchange(send_b, recv_b, 1)
 
+    dense_slope = [spans[i] * sigmoid(raw_s[3, i]) for i in range(SAMPLES)]
+    color_slope = [
+        [share[i] * (shade[c][i] * (1.0 - shade[c][i])) for i in range(SAMPLES)] for c in range(3)
+    ]
+
     def slopes(v, carry):
         for i in range(SAMPLES):
             span = slice(i * lanes, (i + 1) * lanes)
@@ -274,9 +278,9 @@
                 (w_in_t, enc, act_one, slope_one),
                 (w_hidden_t, act_one, act_two, slope_two),
             ):
-                pre = dot(w_t[v], before_s[v, :, span])
-                gate = 0.5 + 0.5 * jnp.tanh(0.5 * pre)
-                slope_s[v, :, span] = gate + pre * gate * (1.0 - gate)
+                half = dot(w_t[v], before_s[v, :, span])
+                turned = jnp.tanh(half)
+                slope_s[v, :, span] = 0.5 * (1.0 + turned + half * (1.0 - turned * turned))
         return carry
 
     owner_hot = one_hot(n_vol, owner).astype(BF16)
@@ -327,10 +331,8 @@
     later = through * cots[12:16]
     for i in reversed(range(SAMPLES)):
         pull = sum(cot_color[c] * shade[c][i] for c in range(3))
-        cot_raw = [
-            cot_color[c] * share[i] * (shade[c][i] * (1.0 - shade[c][i])) for c in range(3)
-        ]
-        cot_raw.append((clear[i] * pull - later) * spans[i] * dense_slope[i])
+        cot_raw = [cot_color[c] * color_slope[c][i] for c in range(3)]
+        cot_raw.append((clear[i] * pull - later) * dense_slope[i])
         later = later + share[i] * pull
         for c in range(4):
             for v in range(HELD):

time: 57.3 us -> 56.5 us (0.986)
  Pallas kernels: 56.5 us -> 55.7 us
    pallas_call x1, Pallas kernels: 55 us -> 54.2 us  [local(): pl.pallas_call(functools.partial(kernel, n_rep, n_vol, rays), out_shape=s...]
where the time goes in v4:
time: 56.5 us; the launch traced here: 56.3 us
  Pallas kernels  55.7 us (99%)
  between operations  0.64 us (1%)
    pallas_call x1, Pallas kernels, local(): pl.pallas_call(functools.partial(kernel, n_rep, n_vol, rays), out_shape=s...  54.2 us
    pallas_call x1, Pallas kernels, local(): pl.pallas_call(hand_over, out_shape=shapes, in_specs=[vmem] * 4, out_spec...  1.52 us

profile of v4, /device:TPU:1, one launch (start us, length us, event | category | flops | bytes accessed | tf_op | source)
XLA Modules:
  0.0 56.3 jit_solution(7372805100002071910)
XLA Ops:
  0.6 54.2 %shard_map.102 = (f32[3,256]{1,0:T(4,128)}, f32[4,16,64]{2,1,0:T(8,128)}, f32[4,16,256]{2,1,0:T(8,128)}, f32[4,4,16]{2,1,0:T(4,128)}) custom-call(f32[2,24,256]{2,1,0:T(8,128)} %bitcast.4, f32[2,8,256]{2,1,0:T(8,128)} %bitcast.5, s32[2,256]{1,0:T(2,128)} %bitcast.6, f32[3,256]{1,0:T(4,128)} %target_h.1, bf16[4,64,256]{2,1,0:T(8,128)(2,1)} %w_in_h.1, ...), custom_call_target="tpu_custom_call" | custom-call | tf_op jit(solution)/shard_map/pallas_call | solution.py:444
  54.8 1.5 %shard_map.103 = (f32[3,256]{1,0:T(4,128)}, f32[4,16,64]{2,1,0:T(8,128)}, f32[4,16,256]{2,1,0:T(8,128)}, f32[4,4,16]{2,1,0:T(4,128)}) custom-call(f32[3,256]{1,0:T(4,128)} %get-tuple-element.12.refs_0_, f32[4,16,64]{2,1,0:T(8,128)} %get-tuple-element.13.refs_1_, f32[4,16,256]{2,1,0:T(8,128)} %get-tuple-element.14.refs_2_, f32[4,4,16]{2,1,0:T(4,128)} %get-tuple-element.15.refs_3_), custom_call_target="tpu_custom_call" | custom-call | tf_op jit(solution)/shard_map/pallas_call | solution.py:504

commit v5 on v4

--- a/solution.py
+++ b/solution.py
@@ -237,7 +237,7 @@
                 raw_s[c, i, pl.ds(v, 1), :] = raw[c : c + 1]
         return carry
 
-    lax.fori_loop(0, HELD, forward, 0)
+    lax.fori_loop(0, HELD, forward, 0, unroll=True)
 
     shade = [[sigmoid(raw_s[c, i]) for i in range(SAMPLES)] for c in range(3)]
     spans, share, clear = [], [], []

time: 56.5 us -> 55.3 us (0.979)
  Pallas kernels: 55.7 us -> 54.5 us
    pallas_call x1, Pallas kernels: 54.2 us -> 52.9 us  [local(): pl.pallas_call(functools.partial(kernel, n_rep, n_vol, rays), out_shape=s...]
where the time goes in v5:
time: 55.3 us; the launch traced here: 55.1 us
  Pallas kernels  54.5 us (99%)
  between operations  0.64 us (1%)
    pallas_call x1, Pallas kernels, local(): pl.pallas_call(functools.partial(kernel, n_rep, n_vol, rays), out_shape=s...  52.9 us
    pallas_call x1, Pallas kernels, local(): pl.pallas_call(hand_over, out_shape=shapes, in_specs=[vmem] * 4, out_spec...  1.52 us

profile of v5, /device:TPU:1, one launch (start us, length us, event | category | flops | bytes accessed | tf_op | source)
XLA Modules:
  0.0 55.1 jit_solution(7219298692337553799)
XLA Ops:
  0.6 52.9 %shard_map.102 = (f32[3,256]{1,0:T(4,128)}, f32[4,16,64]{2,1,0:T(8,128)}, f32[4,16,256]{2,1,0:T(8,128)}, f32[4,4,16]{2,1,0:T(4,128)}) custom-call(f32[2,24,256]{2,1,0:T(8,128)} %bitcast.4, f32[2,8,256]{2,1,0:T(8,128)} %bitcast.5, s32[2,256]{1,0:T(2,128)} %bitcast.6, f32[3,256]{1,0:T(4,128)} %target_h.1, bf16[4,64,256]{2,1,0:T(8,128)(2,1)} %w_in_h.1, ...), custom_call_target="tpu_custom_call" | custom-call | tf_op jit(solution)/shard_map/pallas_call | solution.py:444
  53.6 1.5 %shard_map.103 = (f32[3,256]{1,0:T(4,128)}, f32[4,16,64]{2,1,0:T(8,128)}, f32[4,16,256]{2,1,0:T(8,128)}, f32[4,4,16]{2,1,0:T(4,128)}) custom-call(f32[3,256]{1,0:T(4,128)} %get-tuple-element.12.refs_0_, f32[4,16,64]{2,1,0:T(8,128)} %get-tuple-element.13.refs_1_, f32[4,16,256]{2,1,0:T(8,128)} %get-tuple-element.14.refs_2_, f32[4,4,16]{2,1,0:T(4,128)} %get-tuple-element.15.refs_3_), custom_call_target="tpu_custom_call" | custom-call | tf_op jit(solution)/shard_map/pallas_call | solution.py:504
